TPU v7x, 32 devices: a whole 2x2x4 slice. The times are simulated.
32 devices in a mesh: dp: 2 (over x), expert: 4 (over y, core), mp: 4 (over z).
Axes of the slice: x: 2, y: 2, z: 4, core: 2. Of those that a mesh axis runs over, the one named last changes fastest.
Arguments:
- tokens: bfloat16 [128, 3072], P('dp'), may hold values from -6 to 6
- expert_ids: int32 [128, 2], P('dp'), may hold values from 0 to 3, all different within a row; in each aligned block of 64 rows (0 to 63, 64 to 127, ...) at most 64 rows name the same one
- gate_values: float32 [128, 2], P('dp'), may hold values from 0.2 to 1
- targets: int32 [128], P('dp'), may hold values from 0 to 32767
- w_gate: bfloat16 [4, 3072, 4, 2048], P('expert', None, 'mp', 'dp'), may hold values from -0.109375 to 0.109375
- w_up: bfloat16 [4, 3072, 4, 2048], P('expert', None, 'mp', 'dp'), may hold values from -0.109375 to 0.109375
- w_down: bfloat16 [4, 4, 2048, 3072], P('expert', 'mp', None, 'dp'), may hold values from -0.0625 to 0.0625
- norm_gain: float32 [3072], replicated, may hold values from 0.1 to 1.9
- lens_head: bfloat16 [3072, 32768], P('dp', ('expert', 'mp')), may hold values from -120 to 120
Outputs:
- mixed: bfloat16 [128, 3072], P('dp')
- log_probs: float32 [128], P('dp')
Inputs may be any that keep to these rules, and one draw needn't show every extreme that they name: `expert_ids`: each row names two different experts; in each aligned block of 64 rows no expert is named by more than 64 rows, a bound that some block reaches.
All inputs are finite; a program needn't handle non-finite values.
Results may differ from a plain program's by a relative error of at most 0.0041.
Values may be sent and summed in bfloat16 or wider, within the bound.
A program may use at most 128 MiB of HBM per device.

v0:
```python
import jax
import jax.numpy as jnp
from jax import lax
from jax.sharding import PartitionSpec as P

f32, bf16 = (jnp.float32, jnp.bfloat16)


def per_device(
    tokens, expert_ids, gate_values, targets, w_gate, w_up, w_down, norm_gain, lens_head
):
    rows, feats = tokens.shape
    owner = lax.axis_index("expert")
    weights = jnp.sum(jnp.where(expert_ids == owner, gate_values, f32(0.0)), axis=1)
    gate_mat = w_gate.reshape(feats, -1)
    up_mat = w_up.reshape(feats, -1)
    down_mat = w_down.reshape(w_down.shape[2], w_down.shape[3])
    own_feats = down_mat.shape[1]
    all_tokens = lax.all_gather(tokens, "dp", axis=0, tiled=True)
    all_weights = lax.all_gather(weights, "dp", axis=0, tiled=True)
    gate_part = jnp.dot(all_tokens, gate_mat, preferred_element_type=f32)
    up_part = jnp.dot(all_tokens, up_mat, preferred_element_type=f32)
    hidden = (jax.nn.silu(gate_part) * up_part).astype(bf16)
    hidden = lax.all_gather(hidden, "dp", axis=1, tiled=True)
    part = jnp.dot(hidden, down_mat, preferred_element_type=f32) * all_weights[:, None]
    summed = lax.psum(part, ("expert", "mp"))
    first = lax.axis_index("dp") * own_feats
    own_tokens = lax.dynamic_slice_in_dim(all_tokens, first, own_feats, axis=1)
    own_gain = lax.dynamic_slice_in_dim(norm_gain, first, own_feats, axis=0)
    mixed_part = (own_tokens.astype(f32) + summed).astype(bf16)
    mixed = lax.all_to_all(mixed_part, "dp", split_axis=0, concat_axis=1, tiled=True)
    mixed_f = mixed.astype(f32)
    scale = lax.rsqrt(jnp.mean(mixed_f * mixed_f, axis=1) + 1e-05)
    gained = (mixed_part.astype(f32) * own_gain[None, :]).astype(bf16)
    logits_part = jnp.dot(gained, lens_head, preferred_element_type=f32)
    logits = lax.psum_scatter(logits_part, "dp", scatter_dimension=0, tiled=True)
    logits = logits * scale[:, None]
    vocab_cols = lens_head.shape[1]
    vocab_start = (owner * lax.axis_size("mp") + lax.axis_index("mp")) * vocab_cols
    columns = vocab_start + lax.broadcasted_iota(jnp.int32, (1, vocab_cols), 1)
    hit = columns == targets[:, None]
    target_local = jnp.sum(jnp.where(hit, logits, f32(0.0)), axis=1)
    top = jnp.max(logits, axis=1)
    total = jnp.sum(jnp.exp(logits - top[:, None]), axis=1)
    stats = lax.all_gather(jnp.stack([top, total, target_local]), ("expert", "mp"))
    tops, totals, hits = (stats[:, 0], stats[:, 1], stats[:, 2])
    top_all = jnp.max(tops, axis=0)
    exp_total = jnp.sum(totals * jnp.exp(tops - top_all[None, :]), axis=0)
    log_probs = jnp.sum(hits, axis=0) - top_all - jnp.log(exp_total)
    return (mixed, log_probs)


def solution(mesh):
    in_specs = (
        P("dp", None),
        P("dp", None),
        P("dp", None),
        P("dp"),
        P("expert", None, "mp", "dp"),
        P("expert", None, "mp", "dp"),
        P("expert", "mp", None, "dp"),
        P(),
        P("dp", ("expert", "mp")),
    )
    out_specs = (P("dp", None), P("dp"))
    return jax.shard_map(
        per_device, mesh=mesh, in_specs=in_specs, out_specs=out_specs, check_vma=False
    )
```

profile of v0, /device:TPU:0, one launch (start us, length us, event | category | flops | bytes accessed | tf_op | source)
XLA Modules:
  0.0 207.5 jit_solution(1650163457520954662)
XLA Ops:
  7.2 0.0 all-reduce.3.cloned.1.call-start
  7.2 0.0 slice-start
  7.2 13.1 %all_gather.15 = bf16[128,3072]{1,0:T(8,128)(2,1)S(1)} all-gather(bf16[64,3072]{1,0:T(8,128)(2,1)} %param.9), channel_id=1, replica_groups=mesh['dp'=2,'expert'=4,'mp'=4] {'dp'}, dimensions={0}, use_global_device_ids=true | all-gather | bytes 1179648 | tf_op jit(solution)/shard_map/all_gather | solution.py:19
  20.3 3.9 %fusion.4 = f32[128,1024]{1,0:T(8,128)S(1)} fusion(bf16[128,3072]{1,0:T(8,128)(2,1)S(1)} %all_gather.15, bf16[1,3072,1,1024]{3,1,2,0:T(8,128)(2,1)} %param.13), kind=kOutput, calls=%fused_computation.4 | convolution fusion | flops 805306368 | bytes 7602176 | tf_op jit(solution)/shard_map/dot_general | solution.py:21
  24.2 0.0 slice-done
  24.2 0.0 slice-done.1
  24.3 0.0 copy-start.4
  24.3 0.0 copy-start.1
  24.3 0.0 copy-start.2
  24.3 1.1 fusion.12
  25.4 8.2 %all_gather.16 = bf16[128,2048]{1,0:T(8,128)(2,1)S(1)} all-gather(bf16[128,1024]{1,0:T(8,128)(2,1)S(1)} %fusion.12), channel_id=1, replica_groups=mesh['dp'=2,'expert'=4,'mp'=4] {'dp'}, dimensions={1}, use_global_device_ids=true | all-gather | bytes 786432 | tf_op jit(solution)/shard_map/all_gather | solution.py:24
  33.6 0.0 copy-done.4
  33.6 0.6 dynamic-slice
  34.9 0.2 dynamic-update-slice
  35.1 4.9 %all-reduce = f32[128]{0:T(128)S(1)} all-reduce(f32[128]{0:T(128)S(1)} %dynamic-update-slice), channel_id=1, replica_groups=mesh['dp'=2,'expert'=4,'mp'=4] {'dp'}, use_global_device_ids=true, to_apply=%add | all-reduce | flops 128 | bytes 1024
  40.0 4.7 %fusion.6 = f32[128,1536]{1,0:T(8,128)} fusion(bf16[128,2048]{1,0:T(8,128)(2,1)S(1)} %all_gather.16, bf16[1,1,2048,1536]{3,2,1,0:T(8,128)(2,1)} %param.15, f32[128]{0:T(128)S(1)} %all-reduce), kind=kOutput, calls=%fused_computation.6 | convolution fusion | flops 805502976 | bytes 7602688 | tf_op jit(solution)/shard_map/dot_general | solution.py:25
  44.7 0.0 all-reduce.3.cloned.1.call-update
  44.7 0.0 reduce-scatter.2.cloned.1.call-start
  44.8 0.1 dynamic_slice.7
  44.9 93.2 %all-reduce.3.cloned.1.call-done = f32[128,1536]{1,0:T(8,128)} async-done(((f32[128,1536]{1,0:T(8,128)}), f32[128,1536]{1,0:T(8,128)}) %all-reduce.3.cloned.1.call-update) | async-done | bytes 786448 | tf_op jit(solution)/shard_map/psum | solution.py:26
  138.1 1.9 add_convert_fusion
  140.0 4.9 %fusion.15 = f32[128,2048]{1,0:T(8,128)} fusion(bf16[1536,2048]{1,0:T(8,128)(2,1)} %param.17, bf16[128,1536]{1,0:T(8,128)(2,1)} %add_convert_fusion, f32[1536]{0:T(1024)S(1)} %dynamic_slice.7), kind=kOutput, calls=%fused_computation.15 | convolution fusion | flops 805896192 | bytes 7739392 | tf_op jit(solution)/shard_map/dot_general | solution.py:35
  144.9 0.0 reduce-scatter.2.cloned.1.call-update
  145.0 3.5 %all-to-all-start = ((bf16[2,64,1536]{2,1,0:T(8,128)(2,1)}), bf16[2,64,1536]{2,1,0:T(8,128)(2,1)S(1)}, u32[]{:S(2)}, u32[]{:S(2)}) async-start(bf16[2,64,1536]{2,1,0:T(8,128)(2,1)} %bitcast.4), calls=%async_computation | async-start | bytes 786432 | tf_op jit(solution)/shard_map/all_to_all | solution.py:31
  148.5 10.2 %all-to-all-done = bf16[2,64,1536]{2,1,0:T(8,128)(2,1)S(1)} async-done(((bf16[2,64,1536]{2,1,0:T(8,128)(2,1)}), bf16[2,64,1536]{2,1,0:T(8,128)(2,1)S(1)}, u32[]{:S(2)}, u32[]{:S(2)}) %all-to-all-start) | async-done | bytes 393248 | tf_op jit(solution)/shard_map/all_to_all | solution.py:31
  158.6 0.8 copy.16
  159.4 0.2 multiply_reduce_fusion
  159.6 7.2 %reduce-scatter.2.cloned.1.call-done = f32[64,2048]{1,0:T(8,128)} async-done(((f32[128,2048]{1,0:T(8,128)}), f32[64,2048]{1,0:T(8,128)}) %reduce-scatter.2.cloned.1.call-update) | async-done | bytes 524304 | tf_op jit(solution)/shard_map/reduce_scatter | solution.py:36
  166.8 1.2 multiply_reduce_fusion.1
  168.0 1.4 exponential_reduce_fusion
  169.4 30.6 %all-gather.1 = f32[16,3,64]{2,1,0:T(4,128)S(1)} all-gather(f32[1,3,64]{2,1,0:T(4,128)S(1)} %maximum_bitcast_fusion), channel_id=2, replica_groups=mesh['dp'=2,'expert'=4,'mp'=4] {'expert','mp'}, dimensions={0}, use_global_device_ids=true | all-gather | bytes 13056 | tf_op jit(solution)/shard_map/all_gather | solution.py:45
  200.1 0.5 log_subtract_fusion
  (15 shorter events, 0.1 us)
Async XLA Ops:
  7.2 130.9 %all-reduce.3.cloned.1.call-start = ((), (), s32[]{:S(2)}) async-start(), calls=%async_computation.2 | async-start | bytes 1572864 | tf_op jit(solution)/shard_map/psum | solution.py:26
  7.2 17.0 %slice-start = ((s8[6291456]{0:T(1024)(128)(4,1)}), s8[4194304]{0:T(1024)(128)(4,1)S(1)}, s32[]{:S(2)}) async-start(s8[6291456]{0:T(1024)(128)(4,1)} %bitcast.41), calls=%async_computation.4 | async-start | bytes 8388608
  20.3 3.9 %slice-start.1 = ((s8[6291456]{0:T(1024)(128)(4,1)}), s8[2097152]{0:T(1024)(128)(4,1)S(1)}, s32[]{:S(2)}) async-start(s8[6291456]{0:T(1024)(128)(4,1)} %bitcast.41), calls=%async_computation.5 | async-start | bytes 4194304
  24.3 9.3 %copy-start.4 = (u32[32]{0:T(128)S(1)}, u32[32]{0:T(128)}, u32[]{:S(2)}) copy-start(u32[32]{0:T(128)} %constant.40) | copy-start | bytes 388
  24.3 10.5 %copy-start.1 = (f32[64,2]{0,1:T(2,128)S(1)}, f32[64,2]{0,1:T(2,128)}, u32[]{:S(2)}) copy-start(f32[64,2]{0,1:T(2,128)} %param.11) | copy-start | bytes 1540
  24.3 10.5 %copy-start.2 = (s32[64,2]{0,1:T(2,128)S(1)}, s32[64,2]{0,1:T(2,128)}, u32[]{:S(2)}) copy-start(s32[64,2]{0,1:T(2,128)} %param.10) | copy-start | bytes 1540
  40.0 4.8 %copy-start = (f32[3072]{0:T(1024)S(1)}, f32[3072]{0:T(1024)}, u32[]{:S(2)}) copy-start(f32[3072]{0:T(1024)} %param.16) | copy-start | bytes 36868
  44.7 122.0 %reduce-scatter.2.cloned.1.call-start = ((), (), s32[]{:S(2)}) async-start(), calls=%async_computation.3 | async-start | bytes 1572864 | tf_op jit(solution)/shard_map/reduce_scatter | solution.py:36
  44.9 123.1 %copy-start.3 = (s32[64]{0:T(128)S(1)}, s32[64]{0:T(128)}, u32[]{:S(2)}) copy-start(s32[64]{0:T(128)} %param.12) | copy-start | bytes 772
  145.0 13.7 %all-to-all-start = ((bf16[2,64,1536]{2,1,0:T(8,128)(2,1)}), bf16[2,64,1536]{2,1,0:T(8,128)(2,1)S(1)}, u32[]{:S(2)}, u32[]{:S(2)}) async-start(bf16[2,64,1536]{2,1,0:T(8,128)(2,1)} %bitcast.4), calls=%async_computation | async-start | bytes 786432 | tf_op jit(solution)/shard_map/all_to_all | solution.py:31
Sparse Core Ops, SparseCore 0:
  44.9 93.1 all-reduce.2
  145.1 21.6 reduce-scatter.1
where the time goes:
time: 208 us; the launch traced here: 207 us
  waiting for transfers between devices  111 us (53%)
  blocking collectives  56.8 us (27%)
  between operations  14.9 us (7%)
  matrix products  14.6 us (7%)
  other arithmetic  5.39 us (3%)
  starting transfers between devices  3.56 us (2%)
    psum x1, waiting for transfers between devices, per_device(): summed = lax.psum(part, ('expert', 'mp'))  93.2 us
    all_gather x1, blocking collectives, per_device(): lax.all_gather(jnp.stack([top, total, target_local]), ('expert', 'mp'))  30.6 us
    all_gather x1, blocking collectives, per_device(): all_tokens = lax.all_gather(tokens, 'dp', axis=0, tiled=True)  13.1 us
    all_to_all x1, waiting for transfers between devices, per_device(): lax.all_to_all(mixed_part, 'dp', split_axis=0, concat_axis=1, tiled=True)  10.2 us
    all_gather x1, blocking collectives, per_device(): hidden = lax.all_gather(hidden, 'dp', axis=1, tiled=True)  8.17 us
    reduce_scatter x1, waiting for transfers between devices, per_device(): lax.psum_scatter(logits_part, 'dp', scatter_dimension=0, tiled=True)  7.19 us
    unnamed x1, blocking collectives  4.92 us
    dot_general x1, matrix products, per_device(): logits_part = jnp.dot(gained, lens_head, preferred_element_type=f32)  4.91 us
  transfers between devices with their start and end apart: 3, of which 3 were waited for; matrix products, arithmetic and copies ran while one was open for 1% of the time, Pallas kernels for 0%

commit v1 on v0

--- a/solution.py
+++ b/solution.py
@@ -23,7 +23,8 @@
     hidden = (jax.nn.silu(gate_part) * up_part).astype(bf16)
     hidden = lax.all_gather(hidden, "dp", axis=1, tiled=True)
     part = jnp.dot(hidden, down_mat, preferred_element_type=f32) * all_weights[:, None]
-    summed = lax.psum(part, ("expert", "mp"))
+    shards = lax.all_gather(part, ("expert", "mp"), axis=0, tiled=False)
+    summed = shards.sum(axis=0)
     first = lax.axis_index("dp") * own_feats
     own_tokens = lax.dynamic_slice_in_dim(all_tokens, first, own_feats, axis=1)
     own_gain = lax.dynamic_slice_in_dim(norm_gain, first, own_feats, axis=0)

time: 208 us -> 222 us (1.067)
  waiting for transfers between devices: 111 us -> 120 us
  other arithmetic: 5.39 us -> 10.1 us
    all_gather x0 -> x1, waiting for transfers between devices: none -> 102 us  [per_device(): shards = lax.all_gather(part, ('expert', 'mp'), axis=0, tiled=False)]
    psum x1 -> x0, waiting for transfers between devices: 93.2 us -> none  [per_device(): summed = lax.psum(part, ('expert', 'mp'))]
    reduce_sum x0 -> x1, other arithmetic: none -> 5.88 us  [per_device(): summed = shards.sum(axis=0)]
  transfers between devices with their start and end apart: 3 -> 3, of which waited for: 3 -> 3; matrix products, arithmetic and copies ran while one was open for 1% -> 0% of each run, Pallas kernels for 0% -> 0%
where the time goes in v1:
time: 222 us; the launch traced here: 221 us
  waiting for transfers between devices  120 us (54%)
  blocking collectives  56.1 us (25%)
  between operations  14.9 us (7%)
  matrix products  14.6 us (7%)
  other arithmetic  10.1 us (5%)
  starting transfers between devices  3.56 us (2%)
    all_gather x1, waiting for transfers between devices, per_device(): shards = lax.all_gather(part, ('expert', 'mp'), axis=0, tiled=False)  102 us
    all_gather x1, blocking collectives, per_device(): lax.all_gather(jnp.stack([top, total, target_local]), ('expert', 'mp'))  29.9 us
    all_gather x1, blocking collectives, per_device(): all_tokens = lax.all_gather(tokens, 'dp', axis=0, tiled=True)  13.1 us
    all_to_all x1, waiting for transfers between devices, per_device(): lax.all_to_all(mixed_part, 'dp', split_axis=0, concat_axis=1, tiled=True)  11.5 us
    all_gather x1, blocking collectives, per_device(): hidden = lax.all_gather(hidden, 'dp', axis=1, tiled=True)  8.17 us
    reduce_scatter x1, waiting for transfers between devices, per_device(): lax.psum_scatter(logits_part, 'dp', scatter_dimension=0, tiled=True)  6.9 us
    reduce_sum x1, other arithmetic, per_device(): summed = shards.sum(axis=0)  5.88 us
    unnamed x1, blocking collectives  4.92 us
  transfers between devices with their start and end apart: 3, of which 3 were waited for; matrix products, arithmetic and copies ran while one was open for 0% of the time, Pallas kernels for 0%

profile of v1, /device:TPU:0, one launch (start us, length us, event | category | flops | bytes accessed | tf_op | source)
XLA Modules:
  0.0 221.4 jit_solution(6077024228306911753)
XLA Ops:
  7.2 0.0 all-gather.5.cloned.1.call-start
  7.2 0.0 slice-start
  7.2 13.1 %all_gather.21 = bf16[128,3072]{1,0:T(8,128)(2,1)S(1)} all-gather(bf16[64,3072]{1,0:T(8,128)(2,1)} %param.9), channel_id=1, replica_groups=mesh['dp'=2,'expert'=4,'mp'=4] {'dp'}, dimensions={0}, use_global_device_ids=true | all-gather | bytes 1179648 | tf_op jit(solution)/shard_map/all_gather | solution.py:19
  20.3 3.9 %fusion.4 = f32[128,1024]{1,0:T(8,128)S(1)} fusion(bf16[128,3072]{1,0:T(8,128)(2,1)S(1)} %all_gather.21, bf16[1,3072,1,1024]{3,1,2,0:T(8,128)(2,1)} %param.13), kind=kOutput, calls=%fused_computation.4 | convolution fusion | flops 805306368 | bytes 7602176 | tf_op jit(solution)/shard_map/dot_general | solution.py:21
  24.2 0.0 slice-done
  24.3 0.0 copy-start.4
  24.3 0.0 copy-start.1
  24.3 0.0 copy-start.2
  24.3 1.1 fusion.12
  25.4 8.2 %all_gather.22 = bf16[128,2048]{1,0:T(8,128)(2,1)S(1)} all-gather(bf16[128,1024]{1,0:T(8,128)(2,1)S(1)} %fusion.12), channel_id=1, replica_groups=mesh['dp'=2,'expert'=4,'mp'=4] {'dp'}, dimensions={1}, use_global_device_ids=true | all-gather | bytes 786432 | tf_op jit(solution)/shard_map/all_gather | solution.py:24
  33.6 0.6 dynamic-slice
  34.9 0.2 dynamic-update-slice
  35.1 4.9 %all-reduce = f32[128]{0:T(128)S(1)} all-reduce(f32[128]{0:T(128)S(1)} %dynamic-update-slice), channel_id=1, replica_groups=mesh['dp'=2,'expert'=4,'mp'=4] {'dp'}, use_global_device_ids=true, to_apply=%add | all-reduce | flops 128 | bytes 1024
  40.0 4.7 %fusion.6 = f32[128,1536]{1,0:T(8,128)} fusion(bf16[128,2048]{1,0:T(8,128)(2,1)S(1)} %all_gather.22, bf16[1,1,2048,1536]{3,2,1,0:T(8,128)(2,1)} %param.15, f32[128]{0:T(128)S(1)} %all-reduce), kind=kOutput, calls=%fused_computation.6 | convolution fusion | flops 805502976 | bytes 7602688 | tf_op jit(solution)/shard_map/dot_general | solution.py:25
  44.7 0.0 all-gather.5.cloned.1.call-update
  44.8 0.0 reduce-scatter.2.cloned.1.call-start
  44.8 0.1 dynamic_slice.7
  44.9 102.0 %all-gather.5.cloned.1.call-done = f32[2048,1536]{1,0:T(8,128)} async-done(((f32[128,1536]{1,0:T(8,128)}), f32[2048,1536]{1,0:T(8,128)}) %all-gather.5.cloned.1.call-update) | async-done | bytes 12582928 | tf_op jit(solution)/shard_map/all_gather | solution.py:26
  146.9 5.9 %reduce_sum.64 = f32[128,1536]{1,0:T(8,128)S(1)} reduce(f32[16,128,1536]{2,1,0:T(8,128)} %bitcast.35, f32[]{:T(128)} %constant.29.clone.1), dimensions={0}, to_apply=%region_1.2 | reduce | flops 2949120 | bytes 13369348 | tf_op jit(solution)/shard_map/reduce_sum | solution.py:27
  152.7 0.0 copy-start.3
  152.8 0.8 add_convert_fusion
  153.6 4.9 %fusion.15 = f32[128,2048]{1,0:T(8,128)} fusion(bf16[1536,2048]{1,0:T(8,128)(2,1)} %param.17, bf16[128,1536]{1,0:T(8,128)(2,1)} %add_convert_fusion, f32[1536]{0:T(1024)S(1)} %dynamic_slice.7), kind=kOutput, calls=%fused_computation.15 | convolution fusion | flops 805896192 | bytes 7739392 | tf_op jit(solution)/shard_map/dot_general | solution.py:36
  158.5 0.0 reduce-scatter.2.cloned.1.call-update
  158.5 3.5 %all-to-all-start = ((bf16[2,64,1536]{2,1,0:T(8,128)(2,1)}), bf16[2,64,1536]{2,1,0:T(8,128)(2,1)S(1)}, u32[]{:S(2)}, u32[]{:S(2)}) async-start(bf16[2,64,1536]{2,1,0:T(8,128)(2,1)} %bitcast.5), calls=%async_computation | async-start | bytes 786432 | tf_op jit(solution)/shard_map/all_to_all | solution.py:32
  162.0 11.5 %all-to-all-done = bf16[2,64,1536]{2,1,0:T(8,128)(2,1)S(1)} async-done(((bf16[2,64,1536]{2,1,0:T(8,128)(2,1)}), bf16[2,64,1536]{2,1,0:T(8,128)(2,1)S(1)}, u32[]{:S(2)}, u32[]{:S(2)}) %all-to-all-start) | async-done | bytes 393248 | tf_op jit(solution)/shard_map/all_to_all | solution.py:32
  173.5 0.8 copy.17
  174.3 0.2 multiply_reduce_fusion
  174.5 6.9 %reduce-scatter.2.cloned.1.call-done = f32[64,2048]{1,0:T(8,128)} async-done(((f32[128,2048]{1,0:T(8,128)}), f32[64,2048]{1,0:T(8,128)}) %reduce-scatter.2.cloned.1.call-update) | async-done | bytes 524304 | tf_op jit(solution)/shard_map/reduce_scatter | solution.py:37
  181.4 1.2 multiply_reduce_fusion.1
  182.7 1.4 exponential_reduce_fusion
  184.1 29.9 %all-gather.2 = f32[16,3,64]{2,1,0:T(4,128)S(1)} all-gather(f32[1,3,64]{2,1,0:T(4,128)S(1)} %maximum_bitcast_fusion), channel_id=3, replica_groups=mesh['dp'=2,'expert'=4,'mp'=4] {'expert','mp'}, dimensions={0}, use_global_device_ids=true | all-gather | bytes 13056 | tf_op jit(solution)/shard_map/all_gather | solution.py:46
  214.1 0.5 log_subtract_fusion
  (16 shorter events, 0.1 us)
Async XLA Ops:
  7.2 139.7 %all-gather.5.cloned.1.call-start = ((), (), s32[]{:S(2)}) async-start(), calls=%async_computation.3 | async-start | bytes 13369344 | tf_op jit(solution)/shard_map/all_gather | solution.py:26
  7.2 17.0 %slice-start = ((s8[6291456]{0:T(1024)(128)(4,1)}), s8[4194304]{0:T(1024)(128)(4,1)S(1)}, s32[]{:S(2)}) async-start(s8[6291456]{0:T(1024)(128)(4,1)} %bitcast.43), calls=%async_computation.4 | async-start | bytes 8388608
  20.3 3.9 %slice-start.1 = ((s8[6291456]{0:T(1024)(128)(4,1)}), s8[2097152]{0:T(1024)(128)(4,1)S(1)}, s32[]{:S(2)}) async-start(s8[6291456]{0:T(1024)(128)(4,1)} %bitcast.43), calls=%async_computation.5 | async-start | bytes 4194304
  24.3 9.3 %copy-start.4 = (u32[32]{0:T(128)S(1)}, u32[32]{0:T(128)}, u32[]{:S(2)}) copy-start(u32[32]{0:T(128)} %constant.40) | copy-start | bytes 388
  24.3 10.5 %copy-start.1 = (f32[64,2]{0,1:T(2,128)S(1)}, f32[64,2]{0,1:T(2,128)}, u32[]{:S(2)}) copy-start(f32[64,2]{0,1:T(2,128)} %param.11) | copy-start | bytes 1540
  24.3 10.5 %copy-start.2 = (s32[64,2]{0,1:T(2,128)S(1)}, s32[64,2]{0,1:T(2,128)}, u32[]{:S(2)}) copy-start(s32[64,2]{0,1:T(2,128)} %param.10) | copy-start | bytes 1540
  40.0 4.8 %copy-start = (f32[3072]{0:T(1024)S(1)}, f32[3072]{0:T(1024)}, u32[]{:S(2)}) copy-start(f32[3072]{0:T(1024)} %param.16) | copy-start | bytes 36868
  44.8 136.6 %reduce-scatter.2.cloned.1.call-start = ((), (), s32[]{:S(2)}) async-start(), calls=%async_computation.2 | async-start | bytes 1572864 | tf_op jit(solution)/shard_map/reduce_scatter | solution.py:37
  152.7 29.9 %copy-start.3 = (s32[64]{0:T(128)S(1)}, s32[64]{0:T(128)}, u32[]{:S(2)}) copy-start(s32[64]{0:T(128)} %param.12) | copy-start | bytes 772
  158.5 15.0 %all-to-all-start = ((bf16[2,64,1536]{2,1,0:T(8,128)(2,1)}), bf16[2,64,1536]{2,1,0:T(8,128)(2,1)S(1)}, u32[]{:S(2)}, u32[]{:S(2)}) async-start(bf16[2,64,1536]{2,1,0:T(8,128)(2,1)} %bitcast.5), calls=%async_computation | async-start | bytes 786432 | tf_op jit(solution)/shard_map/all_to_all | solution.py:32
Sparse Core Ops, SparseCore 0:
  44.9 101.9 all-gather.4
  158.6 22.7 reduce-scatter.1
